TPU v7x, 256 devices: a whole 4x4x8 slice. The times are simulated.
256 devices in a mesh: tp: 8 (over y, core), ad: 32 (over x, z).
Axes of the slice: x: 4, y: 4, z: 8, core: 2. Of those that a mesh axis runs over, the one named last changes fastest.
Arguments:
- hidden: bfloat16 [8192, 8192], P('ad'), may hold values from -6 to 6
- key_value_weight: bfloat16 [8192, 2048], P(None, 'tp'), may hold values from -0.0625 to 0.0625
- request_group: int32 [8192, 1], P('ad'), may hold values from 0 to 31; in each aligned block of 256 rows (0 to 255, 256 to 511, ...) at most 16 rows name the same one
- request_member: int32 [8192], P('ad'), may hold values from 0 to 3
- adapter_down_weight: bfloat16 [8192, 8192], P('tp', 'ad'), may hold values from -0.0625 to 0.0625
- adapter_up_weight: bfloat16 [8192, 2048], P('ad', 'tp'), may hold values from -0.75 to 0.75
Outputs:
- kv_out: bfloat16 [8192, 2048], P('ad', 'tp')
Inputs may be any that keep to these rules, and one draw needn't show every extreme that they name: `request_group`: among the 256 rows of one index of ad, no group is named by more than 16 rows, a bound that some block reaches.
All inputs are finite; a program needn't handle non-finite values.
Results may differ from a plain program's by a relative error of at most 0.007.
Values may be sent and summed in bfloat16 or wider, within the bound.
A program may use at most 128 MiB of HBM per device.

v0:
```python
import jax
import jax.numpy as jnp
from jax import lax
from jax.sharding import PartitionSpec as P

ADAPTER_RANK = 64


def shards(
    hidden, key_value_weight, request_group, request_member, adapter_down_weight, adapter_up_weight
):
    column_portion = adapter_down_weight.shape[0]
    adapter_pool_count = adapter_down_weight.shape[1] // ADAPTER_RANK
    base_output = jnp.dot(hidden, key_value_weight, preferred_element_type=jnp.float32)
    own_cols = lax.dynamic_slice_in_dim(
        hidden, lax.axis_index("tp") * column_portion, column_portion, 1
    )
    owner_index = request_group[:, 0]
    adapter = owner_index * adapter_pool_count + request_member
    block_portion = lax.all_gather(adapter_down_weight, "ad", axis=1, tiled=True)
    column_total = block_portion.shape[1]
    scores = jnp.dot(own_cols, block_portion, preferred_element_type=jnp.float32)
    column = jnp.arange(column_total, dtype=jnp.int32)
    kept_mask = (column // ADAPTER_RANK)[None, :] == adapter[:, None]
    selector = (
        (column % ADAPTER_RANK)[:, None] == jnp.arange(ADAPTER_RANK, dtype=jnp.int32)[None, :]
    ).astype(jnp.float32)
    partial_ranks = jnp.dot(
        jnp.where(kept_mask, scores, 0.0), selector, precision=lax.Precision.HIGHEST
    )
    rank_values = lax.psum(partial_ranks, "tp").astype(jnp.bfloat16)
    block_portion = lax.all_gather(adapter_up_weight, "ad", axis=0, tiled=True)
    line_total = block_portion.shape[0]
    row_index = jnp.arange(line_total, dtype=jnp.int32)
    spread = (
        (row_index % ADAPTER_RANK)[None, :] == jnp.arange(ADAPTER_RANK, dtype=jnp.int32)[:, None]
    ).astype(jnp.bfloat16)
    widened = jnp.dot(rank_values, spread, preferred_element_type=jnp.float32)
    kept_mask = (row_index // ADAPTER_RANK)[None, :] == adapter[:, None]
    raised_output = jnp.where(kept_mask, widened, 0.0).astype(jnp.bfloat16)
    adapter_update = jnp.dot(
        raised_output, block_portion, preferred_element_type=jnp.float32
    ).astype(jnp.bfloat16)
    return (base_output + adapter_update.astype(jnp.float32)).astype(jnp.bfloat16)


def solution(mesh):
    placed = (P("ad", None), P(None, "tp"), P("ad", None), P("ad"), P("tp", "ad"), P("ad", "tp"))
    return jax.shard_map(
        shards, mesh=mesh, in_specs=placed, out_specs=P("ad", "tp"), check_vma=False
    )
```

profile of v0, /device:TPU:1, one launch (start us, length us, event | category | flops | bytes accessed | tf_op | source)
XLA Modules:
  0.0 259.7 jit_solution(4664037618094021107)
XLA Ops:
  6.5 0.0 all-gather.3.cloned.1.call-start
  6.5 0.7 all-gather.3.cloned.1.call-update
  7.3 0.0 all-gather.5.cloned.1.call-start
  7.3 0.7 all-gather.5.cloned.1.call-update
  8.0 0.7 broadcast_multiply_fusion
  8.7 0.7 add.34
  9.4 152.5 %all-gather.3.cloned.1.call-done = bf16[1024,8192]{1,0:T(8,128)(2,1)} async-done(((bf16[1024,256]{1,0:T(8,128)(2,1)}), bf16[1024,8192]{1,0:T(8,128)(2,1)}) %all-gather.3.cloned.1.call-update) | async-done | bytes 16777232 | tf_op jit(solution)/shard_map/all_gather | solution.py:20
  161.8 8.3 %convolution_select_fusion.1 = f32[256,8192]{1,0:T(8,128)S(1)} fusion(bf16[1024,8192]{1,0:T(8,128)(2,1)} %all-gather.3.cloned.1.call-done, s32[8192]{0:T(1024)S(1)} %get-tuple-element.6, s32[256]{0:T(256)S(1)} %add.34, bf16[256,8192]{1,0:T(8,128)(2,1)} %param.6, s32[]{:T(128)S(6)} %select_n.40), kind=kOutput, calls=%fused_computation.1 | convolution fusion | flops 4299161600 | bytes 25723908 | tf_op jit(solution)/shard_map/dot_general | solution.py:22
  170.2 4.1 %fusion.1 = f32[256,64]{1,0:T(8,128)S(1)} fusion(f32[256,8192]{1,0:T(8,128)S(1)} %convolution_select_fusion.1, s32[8192]{0:T(1024)S(1)} %get-tuple-element.5), kind=kOutput, calls=%fused_computation.5 | convolution fusion | flops 1611137024 | bytes 8486912 | tf_op jit(solution)/shard_map/dot_general | solution.py:28
  174.3 25.0 %psum.7 = bf16[256,64]{1,0:T(8,128)(2,1)S(1)} all-reduce(f32[256,64]{1,0:T(8,128)S(1)} %fusion.1), channel_id=1, replica_groups=mesh['tp'=8,'ad'=32] {'tp'}, use_global_device_ids=true, to_apply=%region_0.1 | all-reduce | flops 16384 | bytes 98304 | tf_op jit(solution)/shard_map/psum | solution.py:31
  199.3 43.6 %all-gather.5.cloned.1.call-done = bf16[8192,256]{1,0:T(8,128)(2,1)} async-done(((bf16[256,256]{1,0:T(8,128)(2,1)}), bf16[8192,256]{1,0:T(8,128)(2,1)}) %all-gather.5.cloned.1.call-update) | async-done | bytes 4194320 | tf_op jit(solution)/shard_map/all_gather | solution.py:32
  242.9 4.6 %fusion.5 = f32[256,256]{1,0:T(8,128)S(1)} fusion(bf16[8192,256]{1,0:T(8,128)(2,1)} %all-gather.5.cloned.1.call-done, s32[8192]{0:T(1024)S(1)} %get-tuple-element.6, s32[256]{0:T(256)S(1)} %add.34, s32[8192]{0:T(1024)S(1)} %get-tuple-element.5, bf16[256,64]{1,0:T(8,128)(2,1)S(1)} %psum.7), kind=kOutput, calls=%fused_computation.10 | convolution fusion | flops 1349124096 | bytes 4555776 | tf_op jit(solution)/shard_map/dot_general | solution.py:41
  247.5 5.4 %fusion.3 = bf16[256,256]{1,0:T(8,128)(2,1)} fusion(f32[256,256]{1,0:T(8,128)S(1)} %fusion.5, bf16[256,8192]{1,0:T(8,128)(2,1)} %param.6, bf16[8192,256]{1,0:T(8,128)(2,1)} %param.7), kind=kOutput, calls=%fused_computation.8 | convolution fusion | flops 1073872896 | bytes 8781824 | tf_op jit(solution)/shard_map/dot_general | solution.py:14
  (1 shorter events, 0.0 us)
Async XLA Ops:
  6.5 155.3 %all-gather.3.cloned.1.call-start = ((), (), s32[]{:S(2)}) async-start(), calls=%async_computation | async-start | bytes 17301504 | tf_op jit(solution)/shard_map/all_gather | solution.py:20
  7.3 235.6 %all-gather.5.cloned.1.call-start = ((), (), s32[]{:S(2)}) async-start(), calls=%async_computation.1 | async-start | bytes 4325376 | tf_op jit(solution)/shard_map/all_gather | solution.py:32
Sparse Core Ops, SparseCore 0:
  9.8 151.9 all-gather.2
  164.4 78.4 all-gather.4
where the time goes:
time: 262 us; the launch traced here: 260 us
  waiting for transfers between devices  197 us (75%)
  blocking collectives  25 us (10%)
  matrix products  22.4 us (9%)
  between operations  13.4 us (5%)
    all_gather x1, waiting for transfers between devices, shards(): lax.all_gather(adapter_down_weight, 'ad', axis=1, tiled=True)  152 us
    all_gather x1, waiting for transfers between devices, shards(): block_portion = lax.all_gather(adapter_up_weight, 'ad', axis=0, tiled=True)  43.6 us
    psum x1, blocking collectives, shards(): rank_values = lax.psum(partial_ranks, 'tp').astype(jnp.bfloat16)  25 us
    dot_general x1, matrix products, shards(): jnp.dot(own_cols, block_portion, preferred_element_type=jnp.float32)  8.31 us
    dot_general x1, matrix products, shards(): jnp.dot(hidden, key_value_weight, preferred_element_type=jnp.float32)  5.37 us
  transfers between devices with their start and end apart: 2, of which 2 were waited for; matrix products, arithmetic and copies ran while one was open for 5% of the time, Pallas kernels for 0%

commit v1 on v0

v1 whole, which is shorter than its diff:
```python
import functools

import jax
import jax.numpy as jnp
from jax import lax
from jax.experimental import pallas as pl
from jax.experimental.pallas import tpu as pltpu
from jax.sharding import PartitionSpec as P

RANK = 64
SLOTS = 16
F32 = jnp.float32
BF16 = jnp.bfloat16
MESH = pl.DeviceIdType.MESH


def iota(shape, axis):
    return lax.broadcasted_iota(jnp.int32, shape, axis)


def kernel(
    nx, nz, ntp, hidden, weight, group, member, down, up, out,
    hcols, hbuf, wbuf, dbuf, ubuf, send, recv, meta_out, meta_in,
    part, parts, yout, yin,
    load_sem, base_sem, data_send, data_recv, meta_send, meta_recv,
    part_send, part_recv, ret_send, ret_recv,
):
    rows, depth = hidden.shape
    own = hcols.shape[1]
    wide = nz * SLOTS
    half = wide // 2
    members = dbuf.shape[1] // RANK
    ad = lax.axis_index("ad")
    tp = lax.axis_index("tp")
    x, z = ad // nz, lax.rem(ad, nz)

    def at(dx, dz):
        return {"ad": lax.rem(x + dx + nx, nx) * nz + lax.rem(z + dz + nz, nz)}

    def peer(o):
        return {"tp": lax.rem(tp + o, ntp)}

    offsets = [(dx, dz) for dx in range(nx) for dz in range(nz) if dx or dz]
    barrier = pltpu.get_barrier_semaphore()
    for dx, dz in offsets:
        pl.semaphore_signal(barrier, inc=1, device_id=at(dx, dz), device_id_type=MESH)
    for o in range(1, ntp):
        pl.semaphore_signal(barrier, inc=1, device_id=peer(o), device_id_type=MESH)

    first = pl.multiple_of(tp * own, own)
    loads = [
        pltpu.make_async_copy(hidden.at[:, pl.ds(first, own)], hcols, load_sem.at[0]),
        pltpu.make_async_copy(down, dbuf, load_sem.at[1]),
        pltpu.make_async_copy(up, ubuf, load_sem.at[2]),
    ]
    for load in loads:
        load.start()
    nk = depth // own
    base_loads = []
    for k in range(nk):
        cut = pl.ds(k * own, own)
        base_loads.append((
            pltpu.make_async_copy(hidden.at[:, cut], hbuf.at[k], base_sem.at[0, k]),
            pltpu.make_async_copy(weight.at[cut], wbuf.at[k], base_sem.at[1, k]),
        ))
    for pair in base_loads:
        for load in pair:
            load.start()

    goes = group[...]
    gx, gz = goes // nz, goes % nz
    rel = ((gx - x + nx) % nx) * nz + (gz - z + nz) % nz
    rel_across = rel.astype(F32)
    square = (rows, rows)
    down_at, across_at = iota(square, 0), iota(square, 1)
    rel_down = jnp.sum(jnp.where(down_at == across_at, rel_across, 0.0), axis=1, keepdims=True)
    same = (rel_down == rel_across).astype(F32)
    k_across = jnp.sum(jnp.where(down_at < across_at, same, 0.0), axis=0, keepdims=True)
    k_down = jnp.sum(jnp.where(across_at < down_at, same, 0.0), axis=1, keepdims=True)
    slot_across = (rel_across * SLOTS + k_across).astype(jnp.int32)
    slot_down = (rel_down * SLOTS + k_down).astype(jnp.int32)
    nd = nx * nz
    named = jnp.where(
        iota((nd, rows), 0) == rel_across.astype(jnp.int32), member[...].astype(F32), 0.0
    ).astype(BF16)
    placed = (iota((rows, 128), 1) == k_down.astype(jnp.int32)).astype(F32).astype(BF16)
    meta = jnp.dot(named, placed, preferred_element_type=F32)
    meta_out[...] = meta.reshape(nd, 1, 128)
    meta_in[0] = meta_out[0]

    loads[0].wait()
    mine = hcols[...]
    for c in range(nx):
        pick = (iota((wide, rows), 0) + c * wide == slot_across).astype(F32).astype(BF16)
        send[c] = jnp.dot(pick, mine, preferred_element_type=F32).astype(BF16)
    recv[0, :SLOTS] = send[0, :SLOTS]

    pl.semaphore_wait(barrier, len(offsets) + ntp - 1)

    metas = []
    for dx, dz in offsets:
        i = dx * nz + dz
        metas.append(pltpu.make_async_remote_copy(
            meta_out.at[i], meta_in.at[i], meta_send, meta_recv,
            device_id=at(dx, dz), device_id_type=MESH))
        metas[-1].start()
    order = sorted(range(nz), key=lambda dz: -min(dz, nz - dz))
    for dx in range(nx):
        for dz in order:
            if dx or dz:
                cut = pl.ds(dz * SLOTS, SLOTS)
                pltpu.make_async_remote_copy(
                    send.at[dx, cut], recv.at[dx, cut], data_send.at[dx], data_recv.at[dx],
                    device_id=at(dx, dz), device_id_type=MESH).start()

    base = jnp.zeros((rows, out.shape[1]), F32)
    for k in range(nk):
        for load in base_loads[k]:
            load.wait()
        base = base + jnp.dot(hbuf[k], wbuf[k], preferred_element_type=F32)

    loads[1].wait()
    loads[2].wait()

    def whole(ref, sem):
        return pltpu.make_async_copy(ref, ref, sem)

    whole(meta_in.at[pl.ds(1, nd - 1)], meta_recv).wait()
    left = iota((half, 128), 1) < RANK
    block = iota((wide, members * RANK), 1) // RANK

    def kept(c):
        m = meta_in[c * nz:(c + 1) * nz]
        m = jnp.broadcast_to(m, (nz, SLOTS, 128)).reshape(wide, 128)
        hit = iota((wide, 128), 1) == iota((wide, 128), 0) % SLOTS
        m = jnp.sum(jnp.where(hit, m, 0.0), axis=1, keepdims=True)
        return block == m.astype(jnp.int32)

    def project(c):
        if c == 0:
            whole(recv.at[0, pl.ds(SLOTS, wide - SLOTS)], data_recv.at[0]).wait()
        else:
            whole(recv.at[c], data_recv.at[c]).wait()
        scores = jnp.dot(recv[c], dbuf[...], preferred_element_type=F32)
        scores = jnp.where(kept(c), scores, 0.0)
        total = scores[:, :128]
        for j in range(1, members * RANK // 128):
            total = total + scores[:, j * 128:(j + 1) * 128]
        total = total + pltpu.roll(total, RANK, 1)
        packed = jnp.where(left, total[:half], total[half:])
        part[c] = packed.astype(BF16)
        for o in range(1, ntp):
            pltpu.make_async_remote_copy(
                part.at[c], parts.at[c, o - 1], part_send.at[c], part_recv.at[c],
                device_id=peer(o), device_id_type=MESH).start()
        return packed

    def raise_up(c, packed):
        whole(parts.at[c], part_recv.at[c]).wait()
        total = packed
        for o in range(1, ntp):
            total = total + parts[c, o - 1].astype(F32)
        turned = pltpu.roll(total, RANK, 1)
        both = jnp.concatenate(
            [jnp.where(left, total, turned), jnp.where(left, turned, total)], axis=0)
        spread = jnp.concatenate([both] * (members * RANK // 128), axis=1)
        spread = jnp.where(kept(c), spread, 0.0).astype(BF16)
        yout[c] = jnp.dot(spread, ubuf[...], preferred_element_type=F32).astype(BF16)
        for dz in order:
            if c or dz:
                cut = pl.ds(dz * SLOTS, SLOTS)
                pltpu.make_async_remote_copy(
                    yout.at[c, cut], yin.at[c, cut], ret_send.at[c], ret_recv.at[c],
                    device_id=at(-c, -dz), device_id_type=MESH).start()
            else:
                yin[0, :SLOTS] = yout[0, :SLOTS]

    packed = project(0)
    for c in range(1, nx):
        following = project(c)
        raise_up(c - 1, packed)
        packed = following
    raise_up(nx - 1, packed)

    delta = jnp.zeros((rows, out.shape[1]), F32)
    for c in range(nx):
        cut = yin.at[0, pl.ds(SLOTS, wide - SLOTS)] if c == 0 else yin.at[c]
        whole(cut, ret_recv.at[c]).wait()
        pick = (iota((rows, wide), 1) + c * wide == slot_down).astype(F32).astype(BF16)
        delta = delta + jnp.dot(pick, yin[c], preferred_element_type=F32)
    out[...] = (base + delta).astype(BF16)

    whole(meta_out.at[pl.ds(1, nd - 1)], meta_send).wait()
    for c in range(nx):
        tail = pl.ds(SLOTS, wide - SLOTS)
        whole(send.at[0, tail] if c == 0 else send.at[c], data_send.at[c]).wait()
        whole(yout.at[0, tail] if c == 0 else yout.at[c], ret_send.at[c]).wait()
        whole(parts.at[c], part_send.at[c]).wait()


def build(mesh, nx, nz):
    ntp = mesh.shape["tp"]

    def step(hidden, weight, group, member, down, up):
        rows, depth = hidden.shape
        own, ranks = down.shape
        features = weight.shape[1]
        wide = nz * SLOTS
        nk = depth // own
        nd = nx * nz
        vmem = pl.BlockSpec(memory_space=pltpu.VMEM)
        hbm = pl.BlockSpec(memory_space=pl.ANY)
        dma = pltpu.SemaphoreType.DMA
        return pl.pallas_call(
            functools.partial(kernel, nx, nz, ntp),
            out_shape=jax.ShapeDtypeStruct((rows, features), BF16),
            in_specs=[hbm, hbm, vmem, vmem, hbm, hbm],
            out_specs=vmem,
            scratch_shapes=[
                pltpu.VMEM((rows, own), BF16),
                pltpu.VMEM((nk, rows, own), BF16),
                pltpu.VMEM((nk, own, features), BF16),
                pltpu.VMEM((own, ranks), BF16),
                pltpu.VMEM((ranks, features), BF16),
                pltpu.VMEM((nx, wide, own), BF16),
                pltpu.VMEM((nx, wide, own), BF16),
                pltpu.VMEM((nd, 1, 128), F32),
                pltpu.VMEM((nd, 1, 128), F32),
                pltpu.VMEM((nx, wide // 2, 128), BF16),
                pltpu.VMEM((nx, ntp - 1, wide // 2, 128), BF16),
                pltpu.VMEM((nx, wide, features), BF16),
                pltpu.VMEM((nx, wide, features), BF16),
                dma((3,)), dma((2, nk)), dma((nx,)), dma((nx,)), dma, dma,
                dma((nx,)), dma((nx,)), dma((nx,)), dma((nx,)),
            ],
            compiler_params=pltpu.CompilerParams(
                collective_id=0, has_side_effects=True, vmem_limit_bytes=56 * 1024 * 1024
            ),
        )(hidden, weight, group.reshape(1, rows), member.reshape(1, rows), down, up)

    placed = (P("ad", None), P(None, "tp"), P("ad", None), P("ad"), P("tp", "ad"), P("ad", "tp"))
    return jax.shard_map(
        step, mesh=mesh, in_specs=placed, out_specs=P("ad", "tp"), check_vma=False
    )


def solution(mesh):
    return build(mesh, 4, 8)
```

time: 262 us -> 52.3 us (0.20)
  waiting for transfers between devices: 197 us -> 0 us
  Pallas kernels: 0 us -> 50.6 us
  blocking collectives: 25 us -> 0 us
  matrix products: 22.4 us -> 0 us
  between operations: 13.4 us -> 0.01 us
    all_gather x2 -> x0, waiting for transfers between devices: 196 us -> none  [the longest x1 152 us: shards(): lax.all_gather(adapter_down_weight, 'ad', axis=1, tiled=True)]
    pallas_call x0 -> x1, Pallas kernels: none -> 50.6 us  [step(): pl.pallas_call(functools.partial(kernel, nx, nz, ntp), out_shape=jax.Shap...]
    psum x1 -> x0, blocking collectives: 25 us -> none  [shards(): rank_values = lax.psum(partial_ranks, 'tp').astype(jnp.bfloat16)]
    dot_general x4 -> x0, matrix products: 22.4 us -> none  [the longest x1 8.31 us: shards(): jnp.dot(own_cols, block_portion, preferred_element_type=jnp.float32)]
  transfers between devices with their start and end apart: 2 -> 0, of which waited for: 2 -> 0; matrix products, arithmetic and copies ran while one was open for 5% -> 0% of each run, Pallas kernels for 0% -> 0%
where the time goes in v1:
time: 52.3 us; the launch traced here: 52.2 us
  Pallas kernels  50.6 us (97%)
  local copies, waits for them, and re-layouts  1.57 us (3%)
    pallas_call x1, Pallas kernels, step(): pl.pallas_call(functools.partial(kernel, nx, nz, ntp), out_shape=jax.Shap...  50.6 us
    unnamed x1, local copies, waits for them, and re-layouts  1.57 us

profile of v1, /device:TPU:1, one launch (start us, length us, event | category | flops | bytes accessed | tf_op | source)
XLA Modules:
  0.0 52.2 jit_solution(11760789844250136438)
XLA Ops:
  0.0 50.6 %shard_map.64 = bf16[256,256]{1,0:T(8,128)(2,1)} custom-call(bf16[256,8192]{1,0:T(8,128)(2,1)} %hidden.1, bf16[8192,256]{1,0:T(8,128)(2,1)} %weight.1, s32[1,256]{1,0:T(1,128)} %bitcast.2, s32[1,256]{1,0:T(1,128)} %bitcast.3, bf16[1024,256]{1,0:T(8,128)(2,1)} %down.1, bf16[256,256]{1,0:T(8,128)(2,1)} %up.1), custom_call_target="tpu_custom_call" | custom-call | tf_op jit(solution)/shard_map/pallas_call | solution.py:214
  50.6 1.6 %copy.8 = bf16[256,256]{1,0:T(8,128)(2,1)} copy(bf16[256,256]{1,0:T(8,128)(2,1)} %shard_map.64) | data formatting | bytes 262144

commit v2 on v1

v2 whole, which is shorter than its diff:
```python
import functools

import jax
import jax.numpy as jnp
from jax import lax
from jax.experimental import pallas as pl
from jax.experimental.pallas import tpu as pltpu
from jax.sharding import PartitionSpec as P

RANK = 64
SLOTS = 16
F32 = jnp.float32
BF16 = jnp.bfloat16
CHUNKS = ((0, 12), (12, 20), (20, 28), (28, 32))
MESH = pl.DeviceIdType.MESH


def iota(shape, axis):
    return lax.broadcasted_iota(jnp.int32, shape, axis)


def kernel(
    nx, nz, ntp, chunks, hidden, weight, group, member, down, up, out,
    hcols, hbuf, wbuf, dbuf, ubuf, send, recv, meta_out, meta_in,
    part, parts, yout, yin,
    load_sem, base_sem, data_send, data_recv, meta_send, meta_recv,
    part_send, part_recv, ret_send, ret_recv,
):
    rows, depth = hidden.shape
    own = hcols.shape[1]
    members = dbuf.shape[1] // RANK
    ad = lax.axis_index("ad")
    tp = lax.axis_index("tp")
    x, z = ad // nz, lax.rem(ad, nz)

    def at(dx, dz):
        return {"ad": lax.rem(x + dx + nx, nx) * nz + lax.rem(z + dz + nz, nz)}

    def peer(o):
        return {"tp": lax.rem(tp + o, ntp)}

    by_z = [nz // 2] + [d for k in range(nz // 2 - 1, 0, -1) for d in (k, nz - k)] + [0]
    by_x = [nx // 2] + [d for k in range(nx // 2 - 1, 0, -1) for d in (k, nx - k)] + [0]
    spots = [(dx, dz) for dz in by_z for dx in by_x]
    offsets = spots[:-1]
    first = pl.multiple_of(tp * own, own)
    own_load = pltpu.make_async_copy(hidden.at[:, pl.ds(first, own)], hcols, load_sem.at[0])
    own_load.start()

    barrier = pltpu.get_barrier_semaphore()
    for dx, dz in offsets:
        pl.semaphore_signal(barrier, inc=1, device_id=at(dx, dz), device_id_type=MESH)
    for o in range(1, ntp):
        pl.semaphore_signal(barrier, inc=1, device_id=peer(o), device_id_type=MESH)

    goes = group[...]
    gx, gz = goes // nz, goes % nz

    def place(d, n):
        return jnp.where(d > n // 2, (d - n // 2) * 2, jnp.maximum((n // 2 - d) * 2 - 1, 0))

    rel = place((gz - z + nz) % nz, nz) * nx + place((gx - x + nx) % nx, nx)
    rel_across = rel.astype(F32)
    square = (rows, rows)
    down_at, across_at = iota(square, 0), iota(square, 1)
    rel_down = jnp.sum(jnp.where(down_at == across_at, rel_across, 0.0), axis=1, keepdims=True)
    same = (rel_down == rel_across).astype(F32)
    k_across = jnp.sum(jnp.where(down_at < across_at, same, 0.0), axis=0, keepdims=True)
    k_down = jnp.sum(jnp.where(across_at < down_at, same, 0.0), axis=1, keepdims=True)
    slot_across = (rel_across * SLOTS + k_across).astype(jnp.int32)
    slot_down = (rel_down * SLOTS + k_down).astype(jnp.int32)
    nd = nx * nz
    named = jnp.where(
        iota((nd, rows), 0) == rel_across.astype(jnp.int32), member[...].astype(F32), 0.0
    ).astype(BF16)
    placed = (iota((rows, 128), 1) == k_down.astype(jnp.int32)).astype(F32).astype(BF16)
    meta = jnp.dot(named, placed, preferred_element_type=F32)
    meta_out[...] = meta.reshape(nd, 1, 128)
    meta_in[nd - 1] = meta_out[nd - 1]

    own_load.wait()
    mine = hcols[...]
    self_at = (nd - 1) * SLOTS

    def gather(c):
        lo, hi = chunks[c]
        n = (hi - lo) * SLOTS
        pick = (iota((n, rows), 0) + lo * SLOTS == slot_across).astype(F32).astype(BF16)
        send[lo * SLOTS:hi * SLOTS] = jnp.dot(pick, mine, preferred_element_type=F32).astype(BF16)

    def issue(c):
        for i in range(*chunks[c]):
            if i < nd - 1:
                cut = pl.ds(i * SLOTS, SLOTS)
                pltpu.make_async_remote_copy(
                    send.at[cut], recv.at[cut], data_send.at[c], data_recv.at[c],
                    device_id=at(*spots[i]), device_id_type=MESH).start()

    gather(0)
    pl.semaphore_wait(barrier, len(offsets) + ntp - 1)
    issue(0)
    for i, (dx, dz) in enumerate(offsets):
        pltpu.make_async_remote_copy(
            meta_out.at[i], meta_in.at[i], meta_send, meta_recv,
            device_id=at(dx, dz), device_id_type=MESH).start()
    for c in range(1, len(chunks)):
        gather(c)
        issue(c)
    recv[self_at:] = send[self_at:]

    loads = [
        pltpu.make_async_copy(down, dbuf, load_sem.at[1]),
        pltpu.make_async_copy(up, ubuf, load_sem.at[2]),
    ]
    for load in loads:
        load.start()
    nk = depth // own
    base_loads = []
    for k in range(nk):
        cut = pl.ds(k * own, own)
        base_loads.append((
            pltpu.make_async_copy(hidden.at[:, cut], hbuf.at[k], base_sem.at[0, k]),
            pltpu.make_async_copy(weight.at[cut], wbuf.at[k], base_sem.at[1, k]),
        ))
    for pair in base_loads:
        for load in pair:
            load.start()

    base = jnp.zeros((rows, out.shape[1]), F32)
    for k in range(nk):
        for load in base_loads[k]:
            load.wait()
        base = base + jnp.dot(hbuf[k], wbuf[k], preferred_element_type=F32)

    for load in loads:
        load.wait()

    def whole(ref, sem):
        return pltpu.make_async_copy(ref, ref, sem)

    def away(ref, c):
        lo, hi = chunks[c]
        return ref.at[pl.ds(lo * SLOTS, (min(hi, nd - 1) - lo) * SLOTS)]

    whole(meta_in.at[pl.ds(0, nd - 1)], meta_recv).wait()

    def kept(c):
        lo, hi = chunks[c]
        n = (hi - lo) * SLOTS
        m = jnp.broadcast_to(meta_in[lo:hi], (hi - lo, SLOTS, 128)).reshape(n, 128)
        hit = iota((n, 128), 1) == iota((n, 128), 0) % SLOTS
        m = jnp.sum(jnp.where(hit, m, 0.0), axis=1, keepdims=True)
        return iota((n, members * RANK), 1) // RANK == m.astype(jnp.int32)

    def halves(c):
        lo, hi = chunks[c]
        half = (hi - lo) * SLOTS // 2
        return half, lo * SLOTS // 2

    def project(c):
        lo, hi = chunks[c]
        half, first = halves(c)
        keep = kept(c)
        whole(away(recv, c), data_recv.at[c]).wait()
        scores = jnp.dot(recv[lo * SLOTS:hi * SLOTS], dbuf[...], preferred_element_type=F32)
        scores = jnp.where(keep, scores, 0.0)
        total = scores[:, :128]
        for j in range(1, members * RANK // 128):
            total = total + scores[:, j * 128:(j + 1) * 128]
        total = total + pltpu.roll(total, RANK, 1)
        packed = jnp.where(iota((half, 128), 1) < RANK, total[:half], total[half:])
        part[first:first + half] = packed.astype(BF16)
        for o in range(1, ntp):
            pltpu.make_async_remote_copy(
                part.at[pl.ds(first, half)],
                parts.at[pl.ds(first * (ntp - 1) + (o - 1) * half, half)],
                part_send.at[c], part_recv.at[c],
                device_id=peer(o), device_id_type=MESH).start()
        return packed, keep

    def landed(c):
        half, first = halves(c)
        return parts.at[pl.ds(first * (ntp - 1), half * (ntp - 1))]

    def raise_up(c, packed, keep):
        lo, hi = chunks[c]
        half, first = halves(c)
        whole(landed(c), part_recv.at[c]).wait()
        total = packed
        for o in range(ntp - 1):
            start = first * (ntp - 1) + o * half
            total = total + parts[start:start + half].astype(F32)
        turned = pltpu.roll(total, RANK, 1)
        left = iota((half, 128), 1) < RANK
        both = jnp.concatenate(
            [jnp.where(left, total, turned), jnp.where(left, turned, total)], axis=0)
        spread = jnp.concatenate([both] * (members * RANK // 128), axis=1)
        spread = jnp.where(keep, spread, 0.0).astype(BF16)
        yout[lo * SLOTS:hi * SLOTS] = jnp.dot(
            spread, ubuf[...], preferred_element_type=F32).astype(BF16)
        for i in range(lo, hi):
            cut = pl.ds(i * SLOTS, SLOTS)
            if i < nd - 1:
                dx, dz = spots[i]
                pltpu.make_async_remote_copy(
                    yout.at[cut], yin.at[cut], ret_send.at[c], ret_recv.at[c],
                    device_id=at(-dx, -dz), device_id_type=MESH).start()
            else:
                yin[self_at:] = yout[self_at:]

    held = [project(c) for c in range(len(chunks))]
    for c, kept_ranks in enumerate(held):
        raise_up(c, *kept_ranks)

    delta = base
    for c, (lo, hi) in enumerate(chunks):
        n = (hi - lo) * SLOTS
        pick = (iota((rows, n), 1) + lo * SLOTS == slot_down).astype(F32).astype(BF16)
        whole(away(yin, c), ret_recv.at[c]).wait()
        delta = delta + jnp.dot(pick, yin[lo * SLOTS:hi * SLOTS], preferred_element_type=F32)
    out[...] = delta.astype(BF16)

    whole(meta_out.at[pl.ds(0, nd - 1)], meta_send).wait()
    for c in range(len(chunks)):
        whole(away(send, c), data_send.at[c]).wait()
        whole(away(yout, c), ret_send.at[c]).wait()
        whole(landed(c), part_send.at[c]).wait()


def build(mesh, nx, nz, chunks):
    ntp = mesh.shape["tp"]

    def step(hidden, weight, group, member, down, up):
        rows, depth = hidden.shape
        own, ranks = down.shape
        features = weight.shape[1]
        nk = depth // own
        nd = nx * nz
        total = nd * SLOTS
        nc = len(chunks)
        vmem = pl.BlockSpec(memory_space=pltpu.VMEM)
        hbm = pl.BlockSpec(memory_space=pl.ANY)
        dma = pltpu.SemaphoreType.DMA
        return pl.pallas_call(
            functools.partial(kernel, nx, nz, ntp, chunks),
            out_shape=jax.ShapeDtypeStruct((rows, features), BF16),
            in_specs=[hbm, hbm, vmem, vmem, hbm, hbm],
            out_specs=vmem,
            scratch_shapes=[
                pltpu.VMEM((rows, own), BF16),
                pltpu.VMEM((nk, rows, own), BF16),
                pltpu.VMEM((nk, own, features), BF16),
                pltpu.VMEM((own, ranks), BF16),
                pltpu.VMEM((ranks, features), BF16),
                pltpu.VMEM((total, own), BF16),
                pltpu.VMEM((total, own), BF16),
                pltpu.VMEM((nd, 1, 128), F32),
                pltpu.VMEM((nd, 1, 128), F32),
                pltpu.VMEM((total // 2, 128), BF16),
                pltpu.VMEM(((ntp - 1) * total // 2, 128), BF16),
                pltpu.VMEM((total, features), BF16),
                pltpu.VMEM((total, features), BF16),
                dma((3,)), dma((2, nk)), dma((nc,)), dma((nc,)), dma, dma,
                dma((nc,)), dma((nc,)), dma((nc,)), dma((nc,)),
            ],
            compiler_params=pltpu.CompilerParams(
                collective_id=0, has_side_effects=True, vmem_limit_bytes=56 * 1024 * 1024
            ),
        )(hidden, weight, group.reshape(1, rows), member.reshape(1, rows), down, up)

    placed = (P("ad", None), P(None, "tp"), P("ad", None), P("ad"), P("tp", "ad"), P("ad", "tp"))
    return jax.shard_map(
        step, mesh=mesh, in_specs=placed, out_specs=P("ad", "tp"), check_vma=False
    )


def solution(mesh):
    return build(mesh, 4, 8, CHUNKS)
```

time: 52.3 us -> 49.8 us (0.952)
  Pallas kernels: 50.6 us -> 48 us
    pallas_call x1, Pallas kernels: 50.6 us -> 48 us  [step(): pl.pallas_call(functools.partial(kernel, nx, nz, ntp, chunks), out_shape=...]
where the time goes in v2:
time: 49.8 us; the launch traced here: 49.6 us
  Pallas kernels  48 us (96%)
  local copies, waits for them, and re-layouts  1.57 us (3%)
    pallas_call x1, Pallas kernels, step(): pl.pallas_call(functools.partial(kernel, nx, nz, ntp, chunks), out_shape=...  48 us
    unnamed x1, local copies, waits for them, and re-layouts  1.57 us

profile of v2, /device:TPU:1, one launch (start us, length us, event | category | flops | bytes accessed | tf_op | source)
XLA Modules:
  0.0 49.6 jit_solution(4836243416206218218)
XLA Ops:
  0.0 48.0 %shard_map.64 = bf16[256,256]{1,0:T(8,128)(2,1)} custom-call(bf16[256,8192]{1,0:T(8,128)(2,1)} %hidden.1, bf16[8192,256]{1,0:T(8,128)(2,1)} %weight.1, s32[1,256]{1,0:T(1,128)} %bitcast.2, s32[1,256]{1,0:T(1,128)} %bitcast.3, bf16[1024,256]{1,0:T(8,128)(2,1)} %down.1, bf16[256,256]{1,0:T(8,128)(2,1)} %up.1), custom_call_target="tpu_custom_call" | custom-call | tf_op jit(solution)/shard_map/pallas_call | solution.py:244
  48.0 1.6 %copy.8 = bf16[256,256]{1,0:T(8,128)(2,1)} copy(bf16[256,256]{1,0:T(8,128)(2,1)} %shard_map.64) | data formatting | bytes 262144

commit v3 on v2

--- a/solution.py
+++ b/solution.py
@@ -11,7 +11,6 @@
 SLOTS = 16
 F32 = jnp.float32
 BF16 = jnp.bfloat16
-CHUNKS = ((0, 12), (12, 20), (20, 28), (28, 32))
 MESH = pl.DeviceIdType.MESH
 
 
@@ -20,11 +19,11 @@
 
 
 def kernel(
-    nx, nz, ntp, chunks, hidden, weight, group, member, down, up, out,
+    nx, nz, ntp, plan, hidden, weight, group, member, down, up, out,
     hcols, hbuf, wbuf, dbuf, ubuf, send, recv, meta_out, meta_in,
     part, parts, yout, yin,
     load_sem, base_sem, data_send, data_recv, meta_send, meta_recv,
-    part_send, part_recv, ret_send, ret_recv,
+    part_send, part_recv, ret_send, ret_recv, ready,
 ):
     rows, depth = hidden.shape
     own = hcols.shape[1]
@@ -39,16 +38,19 @@
     def peer(o):
         return {"tp": lax.rem(tp + o, ntp)}
 
-    by_z = [nz // 2] + [d for k in range(nz // 2 - 1, 0, -1) for d in (k, nz - k)] + [0]
-    by_x = [nx // 2] + [d for k in range(nx // 2 - 1, 0, -1) for d in (k, nx - k)] + [0]
-    spots = [(dx, dz) for dz in by_z for dx in by_x]
+    spots = [spot for chunk in plan for spot in chunk]
+    chunks, nd = [], 0
+    for chunk in plan:
+        chunks.append((nd, nd + len(chunk)))
+        nd += len(chunk)
     offsets = spots[:-1]
     first = pl.multiple_of(tp * own, own)
     own_load = pltpu.make_async_copy(hidden.at[:, pl.ds(first, own)], hcols, load_sem.at[0])
     own_load.start()
 
     barrier = pltpu.get_barrier_semaphore()
-    for dx, dz in offsets:
+    greeted = [(0, dz) for dz in range(1, nz)] + [(dx, 0) for dx in range(1, nx)]
+    for dx, dz in greeted:
         pl.semaphore_signal(barrier, inc=1, device_id=at(dx, dz), device_id_type=MESH)
     for o in range(1, ntp):
         pl.semaphore_signal(barrier, inc=1, device_id=peer(o), device_id_type=MESH)
@@ -56,10 +58,10 @@
     goes = group[...]
     gx, gz = goes // nz, goes % nz
 
-    def place(d, n):
-        return jnp.where(d > n // 2, (d - n // 2) * 2, jnp.maximum((n // 2 - d) * 2 - 1, 0))
-
-    rel = place((gz - z + nz) % nz, nz) * nx + place((gx - x + nx) % nx, nx)
+    code = (gx - x + nx) % nx * nz + (gz - z + nz) % nz
+    rel = jnp.zeros_like(code)
+    for i, (dx, dz) in enumerate(spots):
+        rel = jnp.where(code == dx * nz + dz, i, rel)
     rel_across = rel.astype(F32)
     square = (rows, rows)
     down_at, across_at = iota(square, 0), iota(square, 1)
@@ -69,7 +71,6 @@
     k_down = jnp.sum(jnp.where(across_at < down_at, same, 0.0), axis=1, keepdims=True)
     slot_across = (rel_across * SLOTS + k_across).astype(jnp.int32)
     slot_down = (rel_down * SLOTS + k_down).astype(jnp.int32)
-    nd = nx * nz
     named = jnp.where(
         iota((nd, rows), 0) == rel_across.astype(jnp.int32), member[...].astype(F32), 0.0
     ).astype(BF16)
@@ -96,15 +97,27 @@
                     send.at[cut], recv.at[cut], data_send.at[c], data_recv.at[c],
                     device_id=at(*spots[i]), device_id_type=MESH).start()
 
+    def tell(c):
+        lo, hi = chunks[c]
+        for i in range(lo, min(hi, nd - 1)):
+            pltpu.make_async_remote_copy(
+                meta_out.at[i], meta_in.at[i], meta_send.at[c], meta_recv.at[c],
+                device_id=at(*spots[i]), device_id_type=MESH).start()
+
     gather(0)
-    pl.semaphore_wait(barrier, len(offsets) + ntp - 1)
+    pl.semaphore_wait(barrier, len(greeted) + ntp - 1)
+    for dx in range(1, nx):
+        pl.semaphore_signal(
+            ready.at[nx - dx - 1], inc=1, device_id=at(dx, 0), device_id_type=MESH)
+    tell(0)
     issue(0)
-    for i, (dx, dz) in enumerate(offsets):
-        pltpu.make_async_remote_copy(
-            meta_out.at[i], meta_in.at[i], meta_send, meta_recv,
-            device_id=at(dx, dz), device_id_type=MESH).start()
+    unheard = set(range(1, nx))
     for c in range(1, len(chunks)):
         gather(c)
+        for dx in sorted({dx for dx, dz in plan[c] if dz} & unheard):
+            pl.semaphore_wait(ready.at[dx - 1], 1)
+            unheard.remove(dx)
+        tell(c)
         issue(c)
     recv[self_at:] = send[self_at:]
 
@@ -142,7 +155,9 @@
         lo, hi = chunks[c]
         return ref.at[pl.ds(lo * SLOTS, (min(hi, nd - 1) - lo) * SLOTS)]
 
-    whole(meta_in.at[pl.ds(0, nd - 1)], meta_recv).wait()
+    def told(ref, c):
+        lo, hi = chunks[c]
+        return ref.at[pl.ds(lo, min(hi, nd - 1) - lo)]
 
     def kept(c):
         lo, hi = chunks[c]
@@ -160,6 +175,7 @@
     def project(c):
         lo, hi = chunks[c]
         half, first = halves(c)
+        whole(told(meta_in, c), meta_recv.at[c]).wait()
         keep = kept(c)
         whole(away(recv, c), data_recv.at[c]).wait()
         scores = jnp.dot(recv[lo * SLOTS:hi * SLOTS], dbuf[...], preferred_element_type=F32)
@@ -220,14 +236,14 @@
         delta = delta + jnp.dot(pick, yin[lo * SLOTS:hi * SLOTS], preferred_element_type=F32)
     out[...] = delta.astype(BF16)
 
-    whole(meta_out.at[pl.ds(0, nd - 1)], meta_send).wait()
     for c in range(len(chunks)):
+        whole(told(meta_out, c), meta_send.at[c]).wait()
         whole(away(send, c), data_send.at[c]).wait()
         whole(away(yout, c), ret_send.at[c]).wait()
         whole(landed(c), part_send.at[c]).wait()
 
 
-def build(mesh, nx, nz, chunks):
+def build(mesh, nx, nz, plan):
     ntp = mesh.shape["tp"]
 
     def step(hidden, weight, group, member, down, up):
@@ -237,13 +253,13 @@
         nk = depth // own
         nd = nx * nz
         total = nd * SLOTS
-        nc = len(chunks)
+        nc = len(plan)
         vmem = pl.BlockSpec(memory_space=pltpu.VMEM)
         hbm = pl.BlockSpec(memory_space=pl.ANY)
         dma = pltpu.SemaphoreType.DMA
         return pl.pallas_call(
-            functools.partial(kernel, nx, nz, ntp, chunks),
-            out_shape=jax.ShapeDtypeStruct((rows, features), BF16),
+            functools.partial(kernel, nx, nz, ntp, plan),
+            out_shape=pltpu.VMEM((rows, features), BF16),
             in_specs=[hbm, hbm, vmem, vmem, hbm, hbm],
             out_specs=vmem,
             scratch_shapes=[
@@ -260,8 +276,9 @@
                 pltpu.VMEM(((ntp - 1) * total // 2, 128), BF16),
                 pltpu.VMEM((total, features), BF16),
                 pltpu.VMEM((total, features), BF16),
-                dma((3,)), dma((2, nk)), dma((nc,)), dma((nc,)), dma, dma,
+                dma((3,)), dma((2, nk)), dma((nc,)), dma((nc,)), dma((nc,)), dma((nc,)),
                 dma((nc,)), dma((nc,)), dma((nc,)), dma((nc,)),
+                pltpu.SemaphoreType.REGULAR((nx - 1,)),
             ],
             compiler_params=pltpu.CompilerParams(
                 collective_id=0, has_side_effects=True, vmem_limit_bytes=56 * 1024 * 1024
@@ -274,5 +291,14 @@
     )
 
 
+def plan():
+    far = (4, 3, 5, 2, 6, 1, 7)
+    spots = [(0, dz) for dz in far[:3]] + [(2, 0), (1, 0), (3, 0)]
+    spots += [(dx, dz) for dx in (2, 1, 3) for dz in far]
+    spots += [(0, dz) for dz in far[3:]] + [(0, 0)]
+    ends = (6, 14, 20, 26, 32)
+    return [spots[lo:hi] for lo, hi in zip((0,) + ends, ends)]
+
+
 def solution(mesh):
-    return build(mesh, 4, 8, CHUNKS)
+    return build(mesh, 4, 8, plan())

time: 49.8 us -> 46.3 us (0.930)
  Pallas kernels: 48 us -> 45.5 us
  local copies, waits for them, and re-layouts: 1.57 us -> 0.66 us
    pallas_call x1, Pallas kernels: 48 us -> 45.5 us  [step(): pl.pallas_call(functools.partial(kernel, nx, nz, ntp, plan), out_shape=pl...]
    unnamed x1, local copies, waits for them, and re-layouts: 1.57 us -> 0.66 us
where the time goes in v3:
time: 46.3 us; the launch traced here: 46.2 us
  Pallas kernels  45.5 us (98%)
  local copies, waits for them, and re-layouts  0.66 us (1%)
    pallas_call x1, Pallas kernels, step(): pl.pallas_call(functools.partial(kernel, nx, nz, ntp, plan), out_shape=pl...  45.5 us

profile of v3, /device:TPU:1, one launch (start us, length us, event | category | flops | bytes accessed | tf_op | source)
XLA Modules:
  0.0 46.2 jit_solution(6198889745003943141)
XLA Ops:
  0.0 45.5 %shard_map.64 = bf16[256,256]{1,0:T(8,128)(2,1)S(1)} custom-call(bf16[256,8192]{1,0:T(8,128)(2,1)} %hidden.1, bf16[8192,256]{1,0:T(8,128)(2,1)} %weight.1, s32[1,256]{1,0:T(1,128)} %bitcast.2, s32[1,256]{1,0:T(1,128)} %bitcast.3, bf16[1024,256]{1,0:T(8,128)(2,1)} %down.1, bf16[256,256]{1,0:T(8,128)(2,1)} %up.1), custom_call_target="tpu_custom_call" | custom-call | tf_op jit(solution)/shard_map/pallas_call | solution.py:260
  45.5 0.7 %copy.8 = bf16[256,256]{1,0:T(8,128)(2,1)} copy(bf16[256,256]{1,0:T(8,128)(2,1)S(1)} %shard_map.64) | data formatting | bytes 262144

commit v4 on v3

--- a/solution.py
+++ b/solution.py
@@ -186,7 +186,7 @@
         total = total + pltpu.roll(total, RANK, 1)
         packed = jnp.where(iota((half, 128), 1) < RANK, total[:half], total[half:])
         part[first:first + half] = packed.astype(BF16)
-        for o in range(1, ntp):
+        for o in sorted(range(1, ntp), key=lambda o: -min(o, ntp - o)):
             pltpu.make_async_remote_copy(
                 part.at[pl.ds(first, half)],
                 parts.at[pl.ds(first * (ntp - 1) + (o - 1) * half, half)],
@@ -294,7 +294,7 @@
 def plan():
     far = (4, 3, 5, 2, 6, 1, 7)
     spots = [(0, dz) for dz in far[:3]] + [(2, 0), (1, 0), (3, 0)]
-    spots += [(dx, dz) for dx in (2, 1, 3) for dz in far]
+    spots += [(2, dz) for dz in far] + [(dx, dz) for dz in far for dx in (1, 3)]
     spots += [(0, dz) for dz in far[3:]] + [(0, 0)]
     ends = (6, 14, 20, 26, 32)
     return [spots[lo:hi] for lo, hi in zip((0,) + ends, ends)]

time: 46.3 us -> 46.1 us (level)
  no operation moved by 1% of the time
where the time goes in v4:
time: 46.1 us; the launch traced here: 46 us
  Pallas kernels  45.3 us (98%)
  local copies, waits for them, and re-layouts  0.66 us (1%)
    pallas_call x1, Pallas kernels, step(): pl.pallas_call(functools.partial(kernel, nx, nz, ntp, plan), out_shape=pl...  45.3 us

profile of v4, /device:TPU:1, one launch (start us, length us, event | category | flops | bytes accessed | tf_op | source)
XLA Modules:
  0.0 46.0 jit_solution(17006849138724939830)
XLA Ops:
  0.0 45.3 %shard_map.64 = bf16[256,256]{1,0:T(8,128)(2,1)S(1)} custom-call(bf16[256,8192]{1,0:T(8,128)(2,1)} %hidden.1, bf16[8192,256]{1,0:T(8,128)(2,1)} %weight.1, s32[1,256]{1,0:T(1,128)} %bitcast.2, s32[1,256]{1,0:T(1,128)} %bitcast.3, bf16[1024,256]{1,0:T(8,128)(2,1)} %down.1, bf16[256,256]{1,0:T(8,128)(2,1)} %up.1), custom_call_target="tpu_custom_call" | custom-call | tf_op jit(solution)/shard_map/pallas_call | solution.py:260
  45.3 0.7 %copy.8 = bf16[256,256]{1,0:T(8,128)(2,1)} copy(bf16[256,256]{1,0:T(8,128)(2,1)S(1)} %shard_map.64) | data formatting | bytes 262144

commit v5 on v4

--- a/solution.py
+++ b/solution.py
@@ -296,7 +296,7 @@
     spots = [(0, dz) for dz in far[:3]] + [(2, 0), (1, 0), (3, 0)]
     spots += [(2, dz) for dz in far] + [(dx, dz) for dz in far for dx in (1, 3)]
     spots += [(0, dz) for dz in far[3:]] + [(0, 0)]
-    ends = (6, 14, 20, 26, 32)
+    ends = (6, 14, 20, 26, 30, 32)
     return [spots[lo:hi] for lo, hi in zip((0,) + ends, ends)]
 
 

time: 46.1 us -> 45.7 us (level)
  no operation moved by 1% of the time
where the time goes in v5:
time: 45.7 us; the launch traced here: 45.5 us
  Pallas kernels  44.9 us (98%)
  local copies, waits for them, and re-layouts  0.66 us (1%)
    pallas_call x1, Pallas kernels, step(): pl.pallas_call(functools.partial(kernel, nx, nz, ntp, plan), out_shape=pl...  44.9 us

profile of v5, /device:TPU:1, one launch (start us, length us, event | category | flops | bytes accessed | tf_op | source)
XLA Modules:
  0.0 45.5 jit_solution(5716330659271968488)
XLA Ops:
  0.0 44.9 %shard_map.64 = bf16[256,256]{1,0:T(8,128)(2,1)S(1)} custom-call(bf16[256,8192]{1,0:T(8,128)(2,1)} %hidden.1, bf16[8192,256]{1,0:T(8,128)(2,1)} %weight.1, s32[1,256]{1,0:T(1,128)} %bitcast.2, s32[1,256]{1,0:T(1,128)} %bitcast.3, bf16[1024,256]{1,0:T(8,128)(2,1)} %down.1, bf16[256,256]{1,0:T(8,128)(2,1)} %up.1), custom_call_target="tpu_custom_call" | custom-call | tf_op jit(solution)/shard_map/pallas_call | solution.py:260
  44.9 0.7 %copy.8 = bf16[256,256]{1,0:T(8,128)(2,1)} copy(bf16[256,256]{1,0:T(8,128)(2,1)S(1)} %shard_map.64) | data formatting | bytes 262144
